TPU v7x, 32 devices: a whole 2x2x4 slice. The times are simulated.
32 devices in a mesh: row: 8 (over z, x), col: 4 (over y, core).
Axes of the slice: x: 2, y: 2, z: 4, core: 2. Of those that a mesh axis runs over, the one named last changes fastest.
Arguments:
- points: float32 [2, 2048], P(None, 'row'), may hold values from 0 to 1, as said below
- strip_ids: int32 [2048], P('row'), may hold values from 0 to 3, as said below
- counts: int32 [8], P('row'), may hold values from 128 to 256, as said below
- mode_index: int32 [1024], P('col'), may hold values from 0 to 32767, as said below
- reflectors: float32 [2048, 512], P('row'), may hold values from -0.125 to 0.125
Outputs:
- block_out: float32 [2048, 2048], P('row', 'col')
- upper_out: float32 [128, 2048], P(None, 'col')
Inputs may be any that keep to these rules, and one draw needn't show every extreme that they name: `counts`: an owner's live slots come first among its 256 slots; some owner has all 256 live. `mode_index`: the modes are distinct. `points`: every point lies in the triangle x >= 0, y >= 0, x + y <= 1. `strip_ids`: A slot of owner o has strip o * 4 // 8 or one more, at most 3.
All inputs are finite; a program needn't handle non-finite values.
Results may differ from a plain program's by a relative error of at most 0.0003.
Values sent between devices are 32-bit elements; how exact they have to be, the bound alone decides.
A program may use at most 64 MiB of HBM per device.

v0:
```python
import jax
import jax.numpy as jnp
from jax import lax
from jax.sharding import PartitionSpec as P

PANEL = 128
STRIPS = 4
PRECISE = lax.Precision.HIGHEST
SHIFT_RATE = 1e-06


def spread(array, axis, root):
    mine = lax.axis_index(axis) == root
    return lax.psum(jnp.where(mine, array, jnp.zeros_like(array)), axis)


def product(left, right):
    return jnp.dot(left, right, precision=PRECISE, preferred_element_type=jnp.float32)


def transposed_product(left, right):
    return lax.dot_general(
        left, right, (((0,), (0,)), ((), ())), precision=PRECISE, preferred_element_type=jnp.float32
    )


def cholesky_lower(gram):
    order_ids = jnp.arange(gram.shape[0], dtype=jnp.int32)

    def column_step(column, lower):
        row_now = lax.dynamic_index_in_dim(lower, column, 0, keepdims=False)
        target = lax.dynamic_index_in_dim(gram, column, 1, keepdims=False) - product(lower, row_now)
        pivot = jnp.sqrt(lax.dynamic_index_in_dim(target, column, 0, keepdims=False))
        new_column = jnp.where(order_ids >= column, target / pivot, jnp.zeros_like(target))
        return lax.dynamic_update_slice_in_dim(lower, new_column[:, None], column, 1)

    return lax.fori_loop(0, gram.shape[0], column_step, jnp.zeros_like(gram))


def lower_inverse(lower):
    order_ids = jnp.arange(lower.shape[0], dtype=jnp.int32)

    def row_step(row, inverse):
        row_now = lax.dynamic_index_in_dim(lower, row, 0, keepdims=False)
        unit_row = (order_ids == row).astype(lower.dtype)
        pivot = lax.dynamic_index_in_dim(row_now, row, 0, keepdims=False)
        new_row = (unit_row - product(row_now, inverse)) / pivot
        return lax.dynamic_update_slice_in_dim(inverse, new_row[None, :], row, 0)

    return lax.fori_loop(0, lower.shape[0], row_step, jnp.zeros_like(lower))


def assemble(points, strip_ids, live_mask, mode_index):
    freq_x = (mode_index // 128 - 128).astype(jnp.float32)
    freq_y = (mode_index % 128 + 1).astype(jnp.float32)
    phases = jnp.pi * (points[0][:, None] * freq_x[None, :] + points[1][:, None] * freq_y[None, :])
    weight = 3.0 * jnp.power(10.0, -strip_ids.astype(jnp.float32) / (STRIPS - 1)) * live_mask
    columns_all = jnp.stack([jnp.cos(phases), jnp.sin(phases)], axis=-1).reshape(
        phases.shape[0], -1
    )
    return columns_all * weight[:, None]


def reflect(gram_block, coeffs):
    upper_factor = jnp.triu(gram_block, 1) + 0.5 * jnp.diag(jnp.diagonal(gram_block))
    return product(lower_inverse(upper_factor.T), coeffs)


def orthonormalize(panel_cols):
    gram_one = lax.psum(transposed_product(panel_cols, panel_cols), "row")
    shift_size = SHIFT_RATE * jnp.trace(gram_one)
    lower_one = cholesky_lower(gram_one + shift_size * jnp.eye(PANEL, dtype=jnp.float32))
    basis_one = product(panel_cols, lower_inverse(lower_one).T)
    gram_two = lax.psum(transposed_product(basis_one, basis_one), "row")
    lower_two = cholesky_lower(gram_two)
    basis_cols = product(basis_one, lower_inverse(lower_two).T)
    return (basis_cols, lower_one.T)


def on_device(points, strip_ids, counts, mode_index, reflectors):
    row_count = points.shape[1]
    live_mask = (jnp.arange(row_count, dtype=jnp.int32) < counts[0]).astype(jnp.float32)
    work_block = assemble(points, strip_ids, live_mask, mode_index)
    stored = reflectors * live_mask[:, None]
    panels = stored.shape[1] // PANEL
    shaped = stored.reshape(row_count, panels, PANEL)
    gram_blocks = jnp.einsum(
        "rkp,rkq->kpq", shaped, shaped, precision=PRECISE, preferred_element_type=jnp.float32
    )
    gram_blocks = lax.psum(gram_blocks, "row")

    def apply_panel(panel_step, current):
        columns = lax.dynamic_slice_in_dim(stored, panel_step * PANEL, PANEL, 1)
        coeffs = lax.psum(transposed_product(columns, current), "row")
        gram_block = lax.dynamic_index_in_dim(gram_blocks, panel_step, 0, keepdims=False)
        return current - product(columns, reflect(gram_block, coeffs))

    work_block = lax.fori_loop(0, panels, apply_panel, work_block)
    basis_cols, factor = orthonormalize(work_block[:, :PANEL])
    basis_cols = spread(basis_cols, "col", 0)
    tail_rows = lax.psum(transposed_product(basis_cols, work_block), "row")
    remainder = work_block - product(basis_cols, tail_rows)
    col_count = work_block.shape[1]
    global_col = lax.axis_index("col") * col_count + jnp.arange(col_count, dtype=jnp.int32)
    is_panel = (global_col < PANEL)[None, :]
    norm_scale = jnp.sqrt(jnp.float32(row_count * lax.axis_size("row")))
    padded_basis = jnp.pad(basis_cols, ((0, 0), (0, col_count - PANEL)))
    padded_factor = jnp.pad(factor, ((0, 0), (0, col_count - PANEL)))
    block_out = jnp.where(is_panel, padded_basis * norm_scale, remainder)
    upper_out = jnp.where(is_panel, padded_factor, tail_rows) / norm_scale
    return (block_out, upper_out)


def solution(mesh):
    return jax.shard_map(
        on_device,
        mesh=mesh,
        in_specs=(P(None, "row"), P("row"), P("row"), P("col"), P("row", None)),
        out_specs=(P("row", "col"), P(None, "col")),
        check_vma=False,
    )
```

profile of v0, /device:TPU:0, one launch (start us, length us, event | category | flops | bytes accessed | tf_op | source)
XLA Modules:
  0.0 2036.4 jit_solution(15213815674457690325)
XLA Ops:
  7.9 3.0 fusion.44
  12.3 1.1 fusion.48
  15.9 69.3 %all-reduce.9.cloned.1.call-done = f32[4,128,128]{2,1,0:T(8,128)} async-done(((f32[4,128,128]{2,1,0:T(8,128)}), f32[4,128,128]{2,1,0:T(8,128)}) %all-reduce.9.cloned.1.call-update) | async-done | bytes 262160 | tf_op jit(solution)/shard_map/psum | solution.py:90
  85.2 805.3 %while.115 = (s32[]{:T(128)}, f32[256,512]{1,0:T(8,128)S(1)}, f32[256,512]{1,0:T(8,128)S(1)}, f32[4,128,128]{2,1,0:T(8,128)}, s32[]{:T(128)}, /*index=5*/s32[]{:...) while((s32[]{:T(128)}, f32[256,512]{1,0:T(8,128)S(1)}, ...), condition=%wide.region_5.6_spmd, body=%wide.region_1.5_spmd.sunk | while | flops 503809024 | bytes 5053304 | solution.py:98
  85.3 1.2 fusion.112
  87.4 1.3 gather_fusion
  88.7 195.8 %while.120 = (s32[]{:T(128)}, f32[128,128]{1,0:T(8,128)S(1)}, f32[128,128]{1,0:T(8,128)S(1)}, s32[]{:T(128)}, s32[]{:T(128)}, /*index=5*/s32[]{:T(128)}) while((s32[]{:T(128)}, f32[128,128]{1,0:T(8,128)S(1)}, f32[128,128]{1,0:T(8,128)S(1)}, s32[]{:T(128)}, s32[]{:T(128)}, /*index=5*/s32[]{:T(128)}) %tuple.222), condition=%wide.region_3.3_spmd.clone, body=%wide.region_2.2_spmd.clone.sunk | while | flops 197123 | bytes 69221 | solution.py:50
  284.5 1.3 fusion.113
  286.6 1.2 fusion.112
  288.7 1.3 gather_fusion
  290.1 195.8 %while.120 = (s32[]{:T(128)}, f32[128,128]{1,0:T(8,128)S(1)}, f32[128,128]{1,0:T(8,128)S(1)}, s32[]{:T(128)}, s32[]{:T(128)}, /*index=5*/s32[]{:T(128)}) while((s32[]{:T(128)}, f32[128,128]{1,0:T(8,128)S(1)}, f32[128,128]{1,0:T(8,128)S(1)}, s32[]{:T(128)}, s32[]{:T(128)}, /*index=5*/s32[]{:T(128)}) %tuple.222), condition=%wide.region_3.3_spmd.clone, body=%wide.region_2.2_spmd.clone.sunk | while | flops 197123 | bytes 69221 | solution.py:50
  485.9 1.3 fusion.113
  487.9 1.2 fusion.112
  490.1 1.3 gather_fusion
  491.4 195.8 %while.120 = (s32[]{:T(128)}, f32[128,128]{1,0:T(8,128)S(1)}, f32[128,128]{1,0:T(8,128)S(1)}, s32[]{:T(128)}, s32[]{:T(128)}, /*index=5*/s32[]{:T(128)}) while((s32[]{:T(128)}, f32[128,128]{1,0:T(8,128)S(1)}, f32[128,128]{1,0:T(8,128)S(1)}, s32[]{:T(128)}, s32[]{:T(128)}, /*index=5*/s32[]{:T(128)}) %tuple.222), condition=%wide.region_3.3_spmd.clone, body=%wide.region_2.2_spmd.clone.sunk | while | flops 197123 | bytes 69221 | solution.py:50
  687.2 1.3 fusion.113
  689.3 1.2 fusion.112
  691.4 1.3 gather_fusion
  692.8 195.8 %while.120 = (s32[]{:T(128)}, f32[128,128]{1,0:T(8,128)S(1)}, f32[128,128]{1,0:T(8,128)S(1)}, s32[]{:T(128)}, s32[]{:T(128)}, /*index=5*/s32[]{:T(128)}) while((s32[]{:T(128)}, f32[128,128]{1,0:T(8,128)S(1)}, f32[128,128]{1,0:T(8,128)S(1)}, s32[]{:T(128)}, s32[]{:T(128)}, /*index=5*/s32[]{:T(128)}) %tuple.222), condition=%wide.region_3.3_spmd.clone, body=%wide.region_2.2_spmd.clone.sunk | while | flops 197123 | bytes 69221 | solution.py:50
  888.6 1.3 fusion.113
  890.6 1.0 fusion.51
  891.7 71.6 %all-reduce.11.cloned.1.call-done = f32[128,128]{1,0:T(8,128)} async-done(((f32[128,128]{1,0:T(8,128)}), f32[128,128]{1,0:T(8,128)}) %all-reduce.11.cloned.1.call-update) | async-done | bytes 65552 | tf_op jit(solution)/shard_map/psum | solution.py:70
  963.3 1.5 select_reduce_fusion
  965.6 257.4 %while.116 = (s32[]{:T(128)}, f32[128,128]{1,0:T(8,128)S(1)}, f32[128,128]{0,1:T(8,128)S(1)}, s32[]{:T(128)}, s32[]{:T(128)}) while((s32[]{:T(128)}, f32[128,128]{1,0:T(8,128)S(1)}, f32[128,128]{0,1:T(8,128)S(1)}, s32[]{:T(128)}, s32[]{:T(128)}) %tuple.228), condition=%wide.region_9.10_spmd.clone, body=%wide.region_8.9_spmd.clone.sunk | while | flops 197122 | bytes 71261 | solution.py:37
  1223.0 184.3 %while.117 = (s32[]{:T(128)}, f32[128,128]{1,0:T(8,128)S(1)}, f32[128,128]{1,0:T(8,128)S(1)}, s32[]{:T(128)}, s32[]{:T(128)}, /*index=5*/s32[]{:T(128)}) while((s32[]{:T(128)}, f32[128,128]{1,0:T(8,128)S(1)}, f32[128,128]{1,0:T(8,128)S(1)}, s32[]{:T(128)}, s32[]{:T(128)}, /*index=5*/s32[]{:T(128)}) %tuple.231), condition=%wide.region_11.12_spmd.clone, body=%wide.region_10.11_spmd.clone.sunk | while | flops 197123 | bytes 69221 | solution.py:50
  1408.7 68.5 %all-reduce.13.cloned.1.call-done = f32[128,128]{1,0:T(8,128)} async-done(((f32[128,128]{1,0:T(8,128)}), f32[128,128]{1,0:T(8,128)}) %all-reduce.13.cloned.1.call-update) | async-done | bytes 65552 | tf_op jit(solution)/shard_map/psum | solution.py:74
  1478.1 257.4 %while.118 = (s32[]{:T(128)}, f32[128,128]{1,0:T(8,128)S(1)}, f32[128,128]{0,1:T(8,128)S(1)}, s32[]{:T(128)}, s32[]{:T(128)}) while((s32[]{:T(128)}, f32[128,128]{1,0:T(8,128)S(1)}, f32[128,128]{0,1:T(8,128)S(1)}, s32[]{:T(128)}, s32[]{:T(128)}) %tuple.234), condition=%wide.region_14.15_spmd.clone, body=%wide.region_13.14_spmd.clone.sunk | while | flops 197122 | bytes 71261 | solution.py:37
  1735.5 184.3 %while.119 = (s32[]{:T(128)}, f32[128,128]{1,0:T(8,128)S(1)}, f32[128,128]{1,0:T(8,128)S(1)}, s32[]{:T(128)}, s32[]{:T(128)}, /*index=5*/s32[]{:T(128)}) while((s32[]{:T(128)}, f32[128,128]{1,0:T(8,128)S(1)}, f32[128,128]{1,0:T(8,128)S(1)}, s32[]{:T(128)}, s32[]{:T(128)}, /*index=5*/s32[]{:T(128)}) %tuple.237), condition=%wide.region_16.17_spmd.clone, body=%wide.region_15.16_spmd.clone.sunk | while | flops 197123 | bytes 69221 | solution.py:50
  1920.8 31.4 %all-reduce.15.cloned.1.call-done = f32[256,128]{1,0:T(8,128)} async-done(((f32[256,128]{1,0:T(8,128)}), f32[256,128]{1,0:T(8,128)}) %all-reduce.15.cloned.1.call-update) | async-done | bytes 131088 | tf_op jit(solution)/shard_map/psum | solution.py:14
  1952.2 2.1 fusion.59
  1954.4 72.3 %all-reduce.17.cloned.1.call-done = f32[128,512]{1,0:T(8,128)} async-done(((f32[128,512]{1,0:T(8,128)}), f32[128,512]{1,0:T(8,128)}) %all-reduce.17.cloned.1.call-update) | async-done | bytes 262160 | tf_op jit(solution)/shard_map/psum | solution.py:101
  2026.8 2.4 fusion.43
  (3667 shorter events, 1478.4 us)
Async XLA Ops:
  7.2 78.1 %all-reduce.9.cloned.1.call-start = ((), (), s32[]{:S(2)}) async-start(), calls=%async_computation | async-start | bytes 524288 | tf_op jit(solution)/shard_map/psum | solution.py:90
  10.9 0.7 copy-start.4
  11.6 0.7 copy-start.5
  14.0 0.7 copy-start.6
  14.8 1.0 copy-start
  85.2 199.3 %all-reduce.19.cloned.1.call-start = ((), (), s32[]{:S(2)}) async-start(), calls=%async_computation.5 | async-start | bytes 524288 | tf_op jit(solution)/shard_map/while/body/eval_jaxpr/psum | solution.py:94
  286.5 199.4 %all-reduce.19.cloned.1.call-start = ((), (), s32[]{:S(2)}) async-start(), calls=%async_computation.5 | async-start | bytes 524288 | tf_op jit(solution)/shard_map/while/body/eval_jaxpr/psum | solution.py:94
  487.9 199.4 %all-reduce.19.cloned.1.call-start = ((), (), s32[]{:S(2)}) async-start(), calls=%async_computation.5 | async-start | bytes 524288 | tf_op jit(solution)/shard_map/while/body/eval_jaxpr/psum | solution.py:94
  689.2 199.4 %all-reduce.19.cloned.1.call-start = ((), (), s32[]{:S(2)}) async-start(), calls=%async_computation.5 | async-start | bytes 524288 | tf_op jit(solution)/shard_map/while/body/eval_jaxpr/psum | solution.py:94
  890.6 72.7 %all-reduce.11.cloned.1.call-start = ((), (), s32[]{:S(2)}) async-start(), calls=%async_computation.1 | async-start | bytes 131072 | tf_op jit(solution)/shard_map/psum | solution.py:70
  891.7 585.5 %all-reduce.13.cloned.1.call-start = ((), (), s32[]{:S(2)}) async-start(), calls=%async_computation.2 | async-start | bytes 131072 | tf_op jit(solution)/shard_map/psum | solution.py:74
  963.3 2.2 copy-start.3
  1408.6 543.6 %all-reduce.15.cloned.1.call-start = ((), (), s32[]{:S(2)}) async-start(), calls=%async_computation.3 | async-start | bytes 262144 | tf_op jit(solution)/shard_map/psum | solution.py:14
  1920.8 106.0 %all-reduce.17.cloned.1.call-start = ((), (), s32[]{:S(2)}) async-start(), calls=%async_computation.4 | async-start | bytes 524288 | tf_op jit(solution)/shard_map/psum | solution.py:101
  1954.3 72.5 %copy-start.2 = (f32[256,128]{1,0:T(8,128)S(1)}, f32[256,128]{1,0:T(8,128)}, u32[]{:S(2)}) copy-start(f32[256,128]{1,0:T(8,128)} %all-reduce.15.cloned.1.call-done) | copy-start | bytes 393220
  2026.8 2.4 copy-start.1
Sparse Core Ops, SparseCore 0:
  11.9 73.2 all-reduce.8
  90.4 70.1 all-reduce.18
  291.7 70.0 all-reduce.18
  492.7 70.1 all-reduce.18
  694.1 70.1 all-reduce.18
  895.5 67.7 all-reduce.10
  1408.7 68.4 all-reduce.12
  1920.9 31.2 all-reduce.14
  1956.2 70.5 all-reduce.16
where the time goes:
time: 2060 us; the launch traced here: 2040 us
  local copies, waits for them, and re-layouts  805 us (39%)
  matrix products  693 us (34%)
  waiting for transfers between devices  313 us (15%)
  loops' own time  203 us (10%)
    dot_general x1035, matrix products, product(): jnp.dot(left, right, precision=PRECISE, preferred_element_type=jnp.float32)  682 us
    dynamic_slice x768, local copies, waits for them, and re-layouts, row_step(): pivot = lax.dynamic_index_in_dim(row_now, row, 0, keepdims=False)  484 us
    another operation x2, loops' own time, cholesky_lower(): return lax.fori_loop(0, gram.shape[0], column_step, jnp.zeros_like(gram))  185 us
    dynamic_slice x256, local copies, waits for them, and re-layouts, column_step(): lax.dynamic_index_in_dim(target, column, 0, keepdims=False)  163 us
    dynamic_update_slice x256, local copies, waits for them, and re-layouts, column_step(): lax.dynamic_update_slice_in_dim(lower, new_column[:, None], column, 1)  91.8 us
    psum x1, waiting for transfers between devices, on_device(): tail_rows = lax.psum(transposed_product(basis_cols, work_block), 'row')  72.3 us
    psum x1, waiting for transfers between devices, orthonormalize(): gram_one = lax.psum(transposed_product(panel_cols, panel_cols), 'row')  71.6 us
    psum x1, waiting for transfers between devices, on_device(): gram_blocks = lax.psum(gram_blocks, 'row')  69.3 us
  transfers between devices with their start and end apart: 9, of which 5 were waited for; matrix products, arithmetic and copies ran while one was open for 38% of the time, Pallas kernels for 0%

commit v1 on v0

--- a/solution.py
+++ b/solution.py
@@ -67,7 +67,7 @@
 
 
 def orthonormalize(panel_cols):
-    gram_one = lax.psum(transposed_product(panel_cols, panel_cols), "row")
+    gram_one = jnp.sum(lax.all_gather(transposed_product(panel_cols, panel_cols), "row"), axis=0)
     shift_size = SHIFT_RATE * jnp.trace(gram_one)
     lower_one = cholesky_lower(gram_one + shift_size * jnp.eye(PANEL, dtype=jnp.float32))
     basis_one = product(panel_cols, lower_inverse(lower_one).T)

time: 2060 us -> 1970 us (0.956)
  waiting for transfers between devices: 313 us -> 241 us
  blocking collectives: 0 us -> 31.6 us
  matrix products: 693 us -> 671 us
    psum x1 -> x0, waiting for transfers between devices: 71.6 us -> none  [orthonormalize(): gram_one = lax.psum(transposed_product(panel_cols, panel_cols), 'row')]
    all_gather x0 -> x1, blocking collectives: none -> 31.6 us  [orthonormalize(): lax.all_gather(transposed_product(panel_cols, panel_cols), 'row')]
    dot_general x1035, matrix products: 682 us -> 659 us  [product(): jnp.dot(left, right, precision=PRECISE, preferred_element_type=jnp.float32)]
  transfers between devices with their start and end apart: 9 -> 8, of which waited for: 5 -> 4; matrix products, arithmetic and copies ran while one was open for 38% -> 38% of each run, Pallas kernels for 0% -> 0%
where the time goes in v1:
time: 1970 us; the launch traced here: 1960 us
  local copies, waits for them, and re-layouts  790 us (40%)
  matrix products  671 us (34%)
  waiting for transfers between devices  241 us (12%)
  loops' own time  203 us (10%)
  blocking collectives  31.6 us (2%)
    dot_general x1035, matrix products, product(): jnp.dot(left, right, precision=PRECISE, preferred_element_type=jnp.float32)  659 us
    dynamic_slice x768, local copies, waits for them, and re-layouts, row_step(): pivot = lax.dynamic_index_in_dim(row_now, row, 0, keepdims=False)  469 us
    another operation x2, loops' own time, cholesky_lower(): return lax.fori_loop(0, gram.shape[0], column_step, jnp.zeros_like(gram))  185 us
    dynamic_slice x256, local copies, waits for them, and re-layouts, column_step(): lax.dynamic_index_in_dim(target, column, 0, keepdims=False)  163 us
    dynamic_update_slice x256, local copies, waits for them, and re-layouts, column_step(): lax.dynamic_update_slice_in_dim(lower, new_column[:, None], column, 1)  91.8 us
    psum x1, waiting for transfers between devices, on_device(): tail_rows = lax.psum(transposed_product(basis_cols, work_block), 'row')  72.3 us
    psum x1, waiting for transfers between devices, on_device(): gram_blocks = lax.psum(gram_blocks, 'row')  69.3 us
    psum x1, waiting for transfers between devices, orthonormalize(): gram_two = lax.psum(transposed_product(basis_one, basis_one), 'row')  67.8 us
  transfers between devices with their start and end apart: 8, of which 4 were waited for; matrix products, arithmetic and copies ran while one was open for 38% of the time, Pallas kernels for 0%

profile of v1, /device:TPU:0, one launch (start us, length us, event | category | flops | bytes accessed | tf_op | source)
XLA Modules:
  0.0 1957.3 jit_solution(12882900682431447034)
XLA Ops:
  7.9 3.0 fusion.44
  12.3 1.1 fusion.48
  15.9 69.3 %all-reduce.8.cloned.1.call-done = f32[4,128,128]{2,1,0:T(8,128)} async-done(((f32[4,128,128]{2,1,0:T(8,128)}), f32[4,128,128]{2,1,0:T(8,128)}) %all-reduce.8.cloned.1.call-update) | async-done | bytes 262160 | tf_op jit(solution)/shard_map/psum | solution.py:90
  85.2 768.1 %while.115 = (s32[]{:T(128)}, f32[256,512]{1,0:T(8,128)S(1)}, f32[256,512]{1,0:T(8,128)S(1)}, f32[4,128,128]{2,1,0:T(8,128)}, s32[]{:T(128)}, /*index=5*/s32[]{:...) while((s32[]{:T(128)}, f32[256,512]{1,0:T(8,128)S(1)}, ...), condition=%wide.region_5.6_spmd, body=%wide.region_1.5_spmd.sunk | while | flops 503809024 | bytes 5053304 | solution.py:98
  85.3 1.2 fusion.112
  87.4 1.3 gather_fusion
  88.7 186.5 %while.120 = (s32[]{:T(128)}, f32[128,128]{1,0:T(8,128)S(1)}, f32[128,128]{1,0:T(8,128)S(1)}, s32[]{:T(128)}, s32[]{:T(128)}, /*index=5*/s32[]{:T(128)}) while((s32[]{:T(128)}, f32[128,128]{1,0:T(8,128)S(1)}, f32[128,128]{1,0:T(8,128)S(1)}, s32[]{:T(128)}, s32[]{:T(128)}, /*index=5*/s32[]{:T(128)}) %tuple.222), condition=%wide.region_3.3_spmd.clone, body=%wide.region_2.2_spmd.clone.sunk | while | flops 197123 | bytes 69221 | solution.py:50
  275.2 1.3 fusion.113
  277.3 1.2 fusion.112
  279.4 1.3 gather_fusion
  280.8 186.5 %while.120 = (s32[]{:T(128)}, f32[128,128]{1,0:T(8,128)S(1)}, f32[128,128]{1,0:T(8,128)S(1)}, s32[]{:T(128)}, s32[]{:T(128)}, /*index=5*/s32[]{:T(128)}) while((s32[]{:T(128)}, f32[128,128]{1,0:T(8,128)S(1)}, f32[128,128]{1,0:T(8,128)S(1)}, s32[]{:T(128)}, s32[]{:T(128)}, /*index=5*/s32[]{:T(128)}) %tuple.222), condition=%wide.region_3.3_spmd.clone, body=%wide.region_2.2_spmd.clone.sunk | while | flops 197123 | bytes 69221 | solution.py:50
  467.3 1.3 fusion.113
  469.3 1.2 fusion.112
  471.5 1.3 gather_fusion
  472.8 186.5 %while.120 = (s32[]{:T(128)}, f32[128,128]{1,0:T(8,128)S(1)}, f32[128,128]{1,0:T(8,128)S(1)}, s32[]{:T(128)}, s32[]{:T(128)}, /*index=5*/s32[]{:T(128)}) while((s32[]{:T(128)}, f32[128,128]{1,0:T(8,128)S(1)}, f32[128,128]{1,0:T(8,128)S(1)}, s32[]{:T(128)}, s32[]{:T(128)}, /*index=5*/s32[]{:T(128)}) %tuple.222), condition=%wide.region_3.3_spmd.clone, body=%wide.region_2.2_spmd.clone.sunk | while | flops 197123 | bytes 69221 | solution.py:50
  659.3 1.3 fusion.113
  661.4 1.2 fusion.112
  663.6 1.3 gather_fusion
  664.9 186.5 %while.120 = (s32[]{:T(128)}, f32[128,128]{1,0:T(8,128)S(1)}, f32[128,128]{1,0:T(8,128)S(1)}, s32[]{:T(128)}, s32[]{:T(128)}, /*index=5*/s32[]{:T(128)}) while((s32[]{:T(128)}, f32[128,128]{1,0:T(8,128)S(1)}, f32[128,128]{1,0:T(8,128)S(1)}, s32[]{:T(128)}, s32[]{:T(128)}, /*index=5*/s32[]{:T(128)}) %tuple.222), condition=%wide.region_3.3_spmd.clone, body=%wide.region_2.2_spmd.clone.sunk | while | flops 197123 | bytes 69221 | solution.py:50
  851.4 1.3 fusion.113
  853.8 31.6 %all-gather = f32[1024,128]{1,0:T(8,128)S(1)} all-gather(f32[128,128]{1,0:T(8,128)S(1)} %fusion.51), channel_id=2, replica_groups=mesh['row'=8,'col'=4] {'row'}, dimensions={0}, use_global_device_ids=true | all-gather | bytes 589824 | tf_op jit(solution)/shard_map/all_gather | solution.py:70
  886.9 257.4 %while.116 = (s32[]{:T(128)}, f32[128,128]{1,0:T(8,128)S(1)}, f32[128,128]{0,1:T(8,128)S(1)}, s32[]{:T(128)}, s32[]{:T(128)}) while((s32[]{:T(128)}, f32[128,128]{1,0:T(8,128)S(1)}, f32[128,128]{0,1:T(8,128)S(1)}, s32[]{:T(128)}, s32[]{:T(128)}) %tuple.228), condition=%wide.region_9.10_spmd.clone, body=%wide.region_8.9_spmd.clone.sunk | while | flops 197122 | bytes 71261 | solution.py:37
  1144.3 184.3 %while.117 = (s32[]{:T(128)}, f32[128,128]{1,0:T(8,128)S(1)}, f32[128,128]{1,0:T(8,128)S(1)}, s32[]{:T(128)}, s32[]{:T(128)}, /*index=5*/s32[]{:T(128)}) while((s32[]{:T(128)}, f32[128,128]{1,0:T(8,128)S(1)}, f32[128,128]{1,0:T(8,128)S(1)}, s32[]{:T(128)}, s32[]{:T(128)}, /*index=5*/s32[]{:T(128)}) %tuple.231), condition=%wide.region_11.12_spmd.clone, body=%wide.region_10.11_spmd.clone.sunk | while | flops 197123 | bytes 69221 | solution.py:50
  1328.9 1.0 fusion.58
  1330.0 67.8 %all-reduce.10.cloned.1.call-done = f32[128,128]{1,0:T(8,128)} async-done(((f32[128,128]{1,0:T(8,128)}), f32[128,128]{1,0:T(8,128)}) %all-reduce.10.cloned.1.call-update) | async-done | bytes 65552 | tf_op jit(solution)/shard_map/psum | solution.py:74
  1398.8 257.4 %while.118 = (s32[]{:T(128)}, f32[128,128]{1,0:T(8,128)S(1)}, f32[128,128]{0,1:T(8,128)S(1)}, s32[]{:T(128)}, s32[]{:T(128)}) while((s32[]{:T(128)}, f32[128,128]{1,0:T(8,128)S(1)}, f32[128,128]{0,1:T(8,128)S(1)}, s32[]{:T(128)}, s32[]{:T(128)}) %tuple.234), condition=%wide.region_14.15_spmd.clone, body=%wide.region_13.14_spmd.clone.sunk | while | flops 197122 | bytes 71261 | solution.py:37
  1656.2 184.3 %while.119 = (s32[]{:T(128)}, f32[128,128]{1,0:T(8,128)S(1)}, f32[128,128]{1,0:T(8,128)S(1)}, s32[]{:T(128)}, s32[]{:T(128)}, /*index=5*/s32[]{:T(128)}) while((s32[]{:T(128)}, f32[128,128]{1,0:T(8,128)S(1)}, f32[128,128]{1,0:T(8,128)S(1)}, s32[]{:T(128)}, s32[]{:T(128)}, /*index=5*/s32[]{:T(128)}) %tuple.237), condition=%wide.region_16.17_spmd.clone, body=%wide.region_15.16_spmd.clone.sunk | while | flops 197123 | bytes 69221 | solution.py:50
  1840.4 0.9 convolution_select_fusion
  1841.4 31.4 %all-reduce.12.cloned.1.call-done = f32[256,128]{1,0:T(8,128)} async-done(((f32[256,128]{1,0:T(8,128)}), f32[256,128]{1,0:T(8,128)}) %all-reduce.12.cloned.1.call-update) | async-done | bytes 131088 | tf_op jit(solution)/shard_map/psum | solution.py:14
  1872.8 2.1 fusion.59
  1875.1 72.3 %all-reduce.14.cloned.1.call-done = f32[128,512]{1,0:T(8,128)} async-done(((f32[128,512]{1,0:T(8,128)}), f32[128,512]{1,0:T(8,128)}) %all-reduce.14.cloned.1.call-update) | async-done | bytes 262160 | tf_op jit(solution)/shard_map/psum | solution.py:101
  1947.4 2.4 fusion.43
  (3664 shorter events, 1440.2 us)
Async XLA Ops:
  7.2 78.1 %all-reduce.8.cloned.1.call-start = ((), (), s32[]{:S(2)}) async-start(), calls=%async_computation | async-start | bytes 524288 | tf_op jit(solution)/shard_map/psum | solution.py:90
  10.9 0.7 copy-start.3
  11.6 0.7 copy-start.4
  14.0 0.7 copy-start.5
  14.8 1.0 copy-start
  85.2 190.0 %all-reduce.16.cloned.1.call-start = ((), (), s32[]{:S(2)}) async-start(), calls=%async_computation.4 | async-start | bytes 524288 | tf_op jit(solution)/shard_map/while/body/eval_jaxpr/psum | solution.py:94
  277.2 190.1 %all-reduce.16.cloned.1.call-start = ((), (), s32[]{:S(2)}) async-start(), calls=%async_computation.4 | async-start | bytes 524288 | tf_op jit(solution)/shard_map/while/body/eval_jaxpr/psum | solution.py:94
  469.3 190.1 %all-reduce.16.cloned.1.call-start = ((), (), s32[]{:S(2)}) async-start(), calls=%async_computation.4 | async-start | bytes 524288 | tf_op jit(solution)/shard_map/while/body/eval_jaxpr/psum | solution.py:94
  661.3 190.1 %all-reduce.16.cloned.1.call-start = ((), (), s32[]{:S(2)}) async-start(), calls=%async_computation.4 | async-start | bytes 524288 | tf_op jit(solution)/shard_map/while/body/eval_jaxpr/psum | solution.py:94
  853.4 544.4 %all-reduce.10.cloned.1.call-start = ((), (), s32[]{:S(2)}) async-start(), calls=%async_computation.1 | async-start | bytes 131072 | tf_op jit(solution)/shard_map/psum | solution.py:74
  1329.9 542.9 %all-reduce.12.cloned.1.call-start = ((), (), s32[]{:S(2)}) async-start(), calls=%async_computation.2 | async-start | bytes 262144 | tf_op jit(solution)/shard_map/psum | solution.py:14
  1841.4 106.0 %all-reduce.14.cloned.1.call-start = ((), (), s32[]{:S(2)}) async-start(), calls=%async_computation.3 | async-start | bytes 524288 | tf_op jit(solution)/shard_map/psum | solution.py:101
  1874.9 72.4 %copy-start.2 = (f32[256,128]{1,0:T(8,128)S(1)}, f32[256,128]{1,0:T(8,128)}, u32[]{:S(2)}) copy-start(f32[256,128]{1,0:T(8,128)} %all-reduce.12.cloned.1.call-done) | copy-start | bytes 393220
  1947.4 2.4 copy-start.1
Sparse Core Ops, SparseCore 0:
  11.9 73.2 all-reduce.7
  90.4 70.1 all-reduce.15
  282.4 70.1 all-reduce.15
  474.1 70.0 all-reduce.15
  666.2 70.0 all-reduce.15
  1330.0 67.7 all-reduce.9
  1841.5 31.2 all-reduce.11
  1876.8 70.5 all-reduce.13
